TPU v7x, 256 devices: a whole 4x4x8 slice. The times are simulated.
256 devices in a mesh: member: 8 (over z), band: 32 (over x, y, core).
Axes of the slice: x: 4, y: 4, z: 8, core: 2. Of those that a mesh axis runs over, the one named last changes fastest.
Arguments:
- perturbations: bfloat16 [80, 4, 2, 768, 1536], P('member', None, None, 'band'), may hold values from -0.625 to 0.625
- innovations: float32 [4, 2, 768, 1536], P(None, None, 'band'), may hold values from -6 to 6
- error_weight: float32 [4, 2, 768, 1536], P(None, None, 'band'), may hold values from 1 to 30, as said below
- localization: float32 [256, 128], P('band'), may hold values from 0.5 to 4
Outputs:
- control: float32 [80, 2, 256, 128], P('member', None, 'band')
- residual: float32 [80, 2, 256, 128], P('member', None, 'band')
- increment: float32 [4, 2, 768, 1536], P(None, None, 'band', 'member')
Inputs may be any that keep to these rules, and one draw needn't show every extreme that they name: `error_weight`: positive weights.
All inputs are finite; a program needn't handle non-finite values.
Results may differ from a plain program's by a relative error of at most 0.0003.
Values sent between devices are 32-bit elements; how exact they have to be, the bound alone decides.
No kernel may reach another device: no remote copies, remote signals or barrier semaphores. Data moves between devices by JAX's collectives and lax.ppermute only.
A program may use at most 128 MiB of HBM per device.

v0:
```python
import math

import jax
import jax.numpy as jnp
from jax import lax
from jax.sharding import PartitionSpec as P

NLON = 1536
ZW = 256
MW = 128
VARS = 4
ITERS = 2


HIGHEST_PRECISION = lax.Precision.HIGHEST


def zonal_basis(waves, columns):
    wave_index = jnp.arange(waves, dtype=jnp.int32)
    wave_number = (wave_index + 1) // 2
    column_index = jnp.arange(columns, dtype=jnp.int32)
    product = wave_number[:, None] * column_index[None, :] % columns
    angle = 2.0 * math.pi / columns * product.astype(jnp.float32)
    picked = jnp.where((wave_index % 2 == 0)[:, None], jnp.cos(angle), jnp.sin(angle))
    factor = jnp.where(wave_index == 0, math.sqrt(0.5), 1.0).astype(jnp.float32) * math.sqrt(
        2.0 / columns
    )
    return picked * factor[:, None]


def meridional_basis(rows_total, modes):
    row_index = jnp.arange(rows_total, dtype=jnp.int32)
    mode_index = jnp.arange(modes, dtype=jnp.int32)
    product = mode_index[None, :] * (2 * row_index[:, None] + 1) % (4 * rows_total)
    angle = math.pi / (2.0 * rows_total) * product.astype(jnp.float32)
    factor = jnp.where(mode_index == 0, math.sqrt(0.5), 1.0).astype(jnp.float32) * math.sqrt(
        2.0 / rows_total
    )
    return jnp.cos(angle) * factor[None, :]


def local(perturbations, innovations, error_weight, localization):
    bands = lax.axis_size("band")
    member_count = lax.axis_size("member")
    all_rows = innovations.shape[2] * bands
    zonal = zonal_basis(ZW, NLON)
    merid = meridional_basis(all_rows, MW)
    share_columns = NLON // member_count
    first_column = lax.axis_index("member") * share_columns

    def to_modes(received):
        return (
            jnp.einsum("klzy,ym->klzm", received, merid, precision=HIGHEST_PRECISION) * localization
        )

    def analyse(grid_field):
        projected = jnp.sum(perturbations * grid_field[None], axis=1)
        coeffs = jnp.einsum("klyx,zx->klzy", projected, zonal, precision=HIGHEST_PRECISION)
        return to_modes(lax.all_to_all(coeffs, "band", split_axis=2, concat_axis=3, tiled=True))

    gradient = analyse(error_weight * innovations)
    control = jnp.zeros_like(gradient)
    increment = jnp.zeros(
        (VARS, innovations.shape[1], innovations.shape[2], share_columns), jnp.float32
    )
    residual = gradient

    def squares(vector):
        return lax.psum(jnp.sum(vector * vector), ("member", "band"))

    direction = gradient
    norm_now = squares(residual)
    for iteration in range(ITERS):
        rows_out = jnp.einsum(
            "klzm,ym->klzy", direction * localization, merid, precision=HIGHEST_PRECISION
        )
        amplitude = jnp.einsum(
            "klzy,zx->klyx",
            lax.all_to_all(rows_out, "band", split_axis=3, concat_axis=2, tiled=True),
            zonal,
            precision=HIGHEST_PRECISION,
        )
        partial_sum = jnp.sum(perturbations * amplitude[:, None], axis=0)
        total = lax.psum(partial_sum, "member")
        weighted = error_weight * total
        own_share = lax.dynamic_slice_in_dim(total, first_column, share_columns, 3)
        image = direction + analyse(weighted)
        curve = lax.psum(jnp.sum(direction * image), ("member", "band"))
        step = norm_now / curve
        control = control + step * direction
        increment = increment + step * own_share
        residual = residual - step * image
        norm_next = squares(residual)
        direction = residual + norm_next / norm_now * direction
        norm_now = norm_next
    return (control, residual, increment)


def solution(mesh):
    return jax.shard_map(
        local,
        mesh=mesh,
        in_specs=(
            P("member", None, None, "band", None),
            P(None, None, "band", None),
            P(None, None, "band", None),
            P("band", None),
        ),
        out_specs=(
            P("member", None, "band", None),
            P("member", None, "band", None),
            P(None, None, "band", "member"),
        ),
        check_vma=False,
    )
```

profile of v0, /device:TPU:1, one launch (start us, length us, event | category | flops | bytes accessed | tf_op | source)
XLA Modules:
  0.0 681.4 jit_solution(8583254347714194181)
XLA Ops:
  13.3 8.9 %fusion.22 = f32[10,2,256,24]{2,3,1,0:T(8,128)S(1)} fusion(f32[10,2,24,1536]{3,2,1,0:T(8,128)S(1)} %fusion, f32[256]{0:T(256)S(1)} %fusion.77, s32[256]{0:T(256)S(1)} %and_select_fusion, pred[256]{0:T(512)(128)(4,1)S(1)} %fusion.78), kind=kOutput, calls=%fused_computation.33 | convolution fusion | flops 2269249536 | bytes 3442944 | tf_op jit(solution)/shard_map/klyx,zx->klzy/dot_general | solution.py:58
  29.6 8.6 %all-to-all-start = ((f32[32,1,3840]{2,1,0:T(1,128)}), f32[32,1,3840]{2,1,0:T(1,128)S(1)}, u32[]{:S(2)}, u32[]{:S(2)}) async-start(f32[32,1,3840]{2,1,0:T(1,128)} %reshape.62), calls=%async_computation | async-start | bytes 983040 | tf_op jit(solution)/shard_map/all_to_all | solution.py:59
  38.3 11.2 %all-to-all-done = f32[32,1,3840]{2,1,0:T(1,128)S(1)} async-done(((f32[32,1,3840]{2,1,0:T(1,128)}), f32[32,1,3840]{2,1,0:T(1,128)S(1)}, u32[]{:S(2)}, u32[]{:S(2)}) %all-to-all-start) | async-done | bytes 491552 | tf_op jit(solution)/shard_map/all_to_all | solution.py:59
  68.1 7.0 %reshape.64 = f32[32,1,3840]{2,1,0:T(1,128)S(1)} reshape(f32[768,2,8,10]{3,2,1,0:T(8,128)} %bitcast.89) | data formatting | bytes 983040
  75.0 14.7 %all_to_all.90 = f32[32,1,3840]{2,1,0:T(1,128)S(1)} all-to-all(f32[32,1,3840]{2,1,0:T(1,128)S(1)} %reshape.64), channel_id=1, replica_groups=mesh['member'=8,'band'=32] {'band'}, dimensions={0} | all-to-all | bytes 983040 | tf_op jit(solution)/shard_map/all_to_all | solution.py:79
  91.5 8.5 %reshape.65 = f32[768,2,8,10]{3,2,1,0:T(8,128)} reshape(f32[32,3840]{1,0:T(8,128)S(1)} %reduce.1) | data formatting | bytes 983040
  100.1 6.1 copy.44
  106.2 10.8 %fusion.7 = f32[10,2,24,1536]{3,2,1,0:T(8,128)S(1)} fusion(f32[10,2,32,8,24]{4,3,2,1,0:T(8,128)S(1)} %copy.44, f32[256]{0:T(256)S(1)} %fusion.77, s32[256]{0:T(256)S(1)} %and_select_fusion, pred[256]{0:T(512)(128)(4,1)S(1)} %fusion.78), kind=kOutput, calls=%fused_computation.12 | convolution fusion | flops 2269249536 | bytes 3442944 | tf_op jit(solution)/shard_map/klzy,zx->klyx/dot_general | solution.py:77
  122.3 71.4 %all-reduce.4.cloned.1.call-done = f32[4,2,24,1536]{3,2,1,0:T(8,128)} async-done(((f32[4,2,24,1536]{3,2,1,0:T(8,128)}), f32[4,2,24,1536]{3,2,1,0:T(8,128)}) %all-reduce.4.cloned.1.call-update) | async-done | bytes 1179664 | tf_op jit(solution)/shard_map/psum | solution.py:84
  199.5 8.9 %fusion.25 = f32[10,2,256,24]{2,3,1,0:T(8,128)S(1)} fusion(f32[10,2,24,1536]{3,2,1,0:T(8,128)S(1)} %fusion.2, f32[256]{0:T(256)S(1)} %fusion.77, s32[256]{0:T(256)S(1)} %and_select_fusion, pred[256]{0:T(512)(128)(4,1)S(1)} %fusion.78), kind=kOutput, calls=%fused_computation.34 | convolution fusion | flops 2269249536 | bytes 3442944 | tf_op jit(solution)/shard_map/klyx,zx->klzy/dot_general | solution.py:58
  216.8 22.5 %all_to_all.91 = f32[32,1,3840]{2,1,0:T(1,128)S(1)} all-to-all(f32[32,1,3840]{2,1,0:T(1,128)S(1)} %reshape.66), channel_id=1, replica_groups=mesh['member'=8,'band'=32] {'band'}, dimensions={0} | all-to-all | bytes 983040 | tf_op jit(solution)/shard_map/all_to_all | solution.py:59
  241.1 5.7 reshape.67
  256.6 73.8 %all-reduce = (f32[]{:T(128)}, f32[]{:T(128)}) all-reduce(f32[]{:T(128)} %get-tuple-element.4, f32[]{:T(128)} %get-tuple-element.3), channel_id=1, replica_groups=mesh['member'=8,'band'=32] {'member','band'}, use_global_device_ids=true, to_apply=%region_2.3 | all-reduce | flops 2 | bytes 16 | tf_op jit(solution)/shard_map/psum | solution.py:69
  332.4 73.4 %psum.45 = f32[]{:T(128)} all-reduce(f32[]{:T(128)} %multiply_reduce_fusion.1), channel_id=1, replica_groups=mesh['member'=8,'band'=32] {'member','band'}, use_global_device_ids=true, to_apply=%region_9.10 | all-reduce | flops 1 | bytes 8 | tf_op jit(solution)/shard_map/psum | solution.py:69
  414.4 7.0 %reshape.68 = f32[32,1,3840]{2,1,0:T(1,128)S(1)} reshape(f32[768,2,8,10]{3,2,1,0:T(8,128)} %bitcast.91) | data formatting | bytes 983040
  421.4 15.9 %all_to_all.92 = f32[32,1,3840]{2,1,0:T(1,128)S(1)} all-to-all(f32[32,1,3840]{2,1,0:T(1,128)S(1)} %reshape.68), channel_id=1, replica_groups=mesh['member'=8,'band'=32] {'band'}, dimensions={0} | all-to-all | bytes 983040 | tf_op jit(solution)/shard_map/all_to_all | solution.py:79
  439.1 8.5 %reshape.69 = f32[768,2,8,10]{3,2,1,0:T(8,128)} reshape(f32[32,3840]{1,0:T(8,128)S(1)} %reduce.3) | data formatting | bytes 983040
  447.6 6.9 %copy.51 = f32[10,2,32,8,24]{4,3,2,1,0:T(8,128)} copy(f32[10,2,32,8,24]{0,3,1,4,2:T(8,128)} %bitcast.92) | data formatting | bytes 983040 | tf_op jit(solution)/shard_map/all_to_all | solution.py:79
  454.5 12.5 %fusion.5 = f32[10,2,24,1536]{3,2,1,0:T(8,128)S(1)} fusion(f32[10,2,32,8,24]{4,3,2,1,0:T(8,128)} %copy.51, f32[256]{0:T(256)S(1)} %fusion.77, s32[256]{0:T(256)S(1)} %and_select_fusion, pred[256]{0:T(512)(128)(4,1)S(1)} %fusion.78), kind=kOutput, calls=%fused_computation.10 | convolution fusion | flops 2269249536 | bytes 3442944 | tf_op jit(solution)/shard_map/klzy,zx->klyx/dot_general | solution.py:77
  472.2 68.1 %all-reduce.6.cloned.1.call-done = f32[4,2,24,1536]{3,2,1,0:T(8,128)} async-done(((f32[4,2,24,1536]{3,2,1,0:T(8,128)}), f32[4,2,24,1536]{3,2,1,0:T(8,128)}) %all-reduce.6.cloned.1.call-update) | async-done | bytes 1179664 | tf_op jit(solution)/shard_map/psum | solution.py:84
  546.4 8.9 %fusion.28 = f32[10,2,256,24]{2,3,1,0:T(8,128)S(1)} fusion(f32[10,2,24,1536]{3,2,1,0:T(8,128)S(1)} %fusion.4, f32[256]{0:T(256)S(1)} %fusion.77, s32[256]{0:T(256)S(1)} %and_select_fusion, pred[256]{0:T(512)(128)(4,1)S(1)} %fusion.78), kind=kOutput, calls=%fused_computation.35 | convolution fusion | flops 2269249536 | bytes 3442944 | tf_op jit(solution)/shard_map/klyx,zx->klzy/dot_general | solution.py:58
  562.7 11.4 %all-to-all-start.4 = ((f32[32,1,3840]{2,1,0:T(1,128)}), f32[32,1,3840]{2,1,0:T(1,128)S(1)}, u32[]{:S(2)}, u32[]{:S(2)}) async-start(f32[32,1,3840]{2,1,0:T(1,128)} %reshape.70), calls=%async_computation.4 | async-start | bytes 983040 | tf_op jit(solution)/shard_map/all_to_all | solution.py:59
  574.2 11.3 %all-to-all-done.4 = f32[32,1,3840]{2,1,0:T(1,128)S(1)} async-done(((f32[32,1,3840]{2,1,0:T(1,128)}), f32[32,1,3840]{2,1,0:T(1,128)S(1)}, u32[]{:S(2)}, u32[]{:S(2)}) %all-to-all-start.4) | async-done | bytes 491552 | tf_op jit(solution)/shard_map/all_to_all | solution.py:59
  596.7 73.7 %psum.47 = f32[]{:T(128)} all-reduce(f32[]{:T(128)} %get-tuple-element.10), channel_id=1, replica_groups=mesh['member'=8,'band'=32] {'member','band'}, use_global_device_ids=true, to_apply=%region_14.15 | all-reduce | flops 1 | bytes 8 | tf_op jit(solution)/shard_map/psum | solution.py:88
  (55 shorter events, 106.9 us)
Async XLA Ops:
  29.6 19.9 %all-to-all-start = ((f32[32,1,3840]{2,1,0:T(1,128)}), f32[32,1,3840]{2,1,0:T(1,128)S(1)}, u32[]{:S(2)}, u32[]{:S(2)}) async-start(f32[32,1,3840]{2,1,0:T(1,128)} %reshape.62), calls=%async_computation | async-start | bytes 983040 | tf_op jit(solution)/shard_map/all_to_all | solution.py:59
  38.2 155.5 %all-reduce.4.cloned.1.call-start = ((), (), s32[]{:S(2)}) async-start(), calls=%async_computation.5 | async-start | bytes 2359296 | tf_op jit(solution)/shard_map/psum | solution.py:84
  56.8 1.7 copy-start.1
  122.0 71.7 %copy-start = (f32[4,2,24,1536]{3,2,1,0:T(8,128)S(1)}, f32[4,2,24,1536]{3,2,1,0:T(8,128)}, u32[]{:S(2)}) copy-start(f32[4,2,24,1536]{3,2,1,0:T(8,128)} %param.6) | copy-start | bytes 3538948
  122.1 418.2 %all-reduce.6.cloned.1.call-start = ((), (), s32[]{:S(2)}) async-start(), calls=%async_computation.6 | async-start | bytes 2359296 | tf_op jit(solution)/shard_map/psum | solution.py:84
  562.7 22.7 %all-to-all-start.4 = ((f32[32,1,3840]{2,1,0:T(1,128)}), f32[32,1,3840]{2,1,0:T(1,128)S(1)}, u32[]{:S(2)}, u32[]{:S(2)}) async-start(f32[32,1,3840]{2,1,0:T(1,128)} %reshape.70), calls=%async_computation.4 | async-start | bytes 983040 | tf_op jit(solution)/shard_map/all_to_all | solution.py:59
Sparse Core Ops, SparseCore 0:
  122.2 71.4 all-reduce.3
  472.3 67.8 all-reduce.5
where the time goes:
time: 690 us; the launch traced here: 681 us
  blocking collectives  274 us (40%)
  waiting for transfers between devices  162 us (23%)
  local copies, waits for them, and re-layouts  104 us (15%)
  matrix products  61.9 us (9%)
  other arithmetic  40.6 us (6%)
  starting transfers between devices  20.3 us (3%)
  between operations  18.6 us (3%)
    psum x2, blocking collectives, squares(): return lax.psum(jnp.sum(vector * vector), ('member', 'band'))  147 us
    psum x2, waiting for transfers between devices, local(): total = lax.psum(partial_sum, 'member')  139 us
    psum x1, blocking collectives, local(): curve = lax.psum(jnp.sum(direction * image), ('member', 'band'))  73.7 us
    unnamed x14, local copies, waits for them, and re-layouts  61.8 us
    all_to_all x2, blocking collectives, local(): lax.all_to_all(rows_out, 'band', split_axis=3, concat_axis=2, tiled=True)  30.6 us
    dot_general x3, matrix products, analyse(): jnp.einsum('klyx,zx->klzy', projected, zonal, precision=HIGHEST_PRECISION)  26.8 us
    dot_general x2, matrix products, local(): jnp.einsum('klzy,zx->klyx', lax.all_to_all(rows_out, 'band', split_axis=3...  23.3 us
    all_to_all x1, blocking collectives, analyse(): lax.all_to_all(coeffs, 'band', split_axis=2, concat_axis=3, tiled=True)  22.5 us
  transfers between devices with their start and end apart: 4, of which 4 were waited for; matrix products, arithmetic and copies ran while one was open for 0% of the time, Pallas kernels for 0%

commit v1 on v0

v1 whole, which is shorter than its diff:
```python
import functools
import math

import jax
import jax.numpy as jnp
import ml_dtypes
import numpy as np
from jax import lax
from jax.experimental import pallas as pl
from jax.experimental.pallas import tpu as pltpu
from jax.sharding import PartitionSpec as P

NLON = 1536
NLAT = 768
ZW = 256
MW = 128
VARS = 4
LEV = 2
KLOC = 10
BANDS = 32
RING = 8
ROWS = 24
TILES = 3
LTILES = NLON // 128
SHARE = NLON // RING
CHUNK = TILES * LTILES * 8
SLOTS = TILES * KLOC
VMEM_LIMIT = 40 * 1024 * 1024


def halves(array):
    high = array.astype(np.float32).astype(ml_dtypes.bfloat16)
    low = (array - high.astype(np.float64)).astype(np.float32).astype(ml_dtypes.bfloat16)
    return high, low


@functools.lru_cache(None)
def bases():
    wave = np.arange(ZW)
    number = (wave + 1) // 2
    angle = 2.0 * math.pi / NLON * ((number[:, None] * np.arange(NLON)[None, :]) % NLON)
    zonal = np.where((wave % 2 == 0)[:, None], np.cos(angle), np.sin(angle))
    zonal = zonal * (np.where(wave == 0, math.sqrt(0.5), 1.0) * math.sqrt(2.0 / NLON))[:, None]
    mode, row = np.arange(MW), np.arange(NLAT)
    angle = math.pi / (2.0 * NLAT) * ((mode[None, :] * (2 * row[:, None] + 1)) % (4 * NLAT))
    merid = np.cos(angle) * (np.where(mode == 0, math.sqrt(0.5), 1.0) * math.sqrt(2.0 / NLAT))
    parts = merid.reshape(BANDS, TILES, 8, MW).transpose(1, 0, 2, 3).reshape(TILES, BANDS * 8, MW)
    first = np.concatenate([parts[0], parts[1]], axis=1)
    second = np.concatenate([parts[1], parts[2]], axis=1)
    return {
        "zonal": np.stack(halves(zonal)),
        "zonal_t": np.stack(halves(zonal.T.copy())),
        "merid": np.stack([np.stack(halves(first)), np.stack(halves(second))]),
        "merid_t": np.stack([np.stack(halves(first.T.copy())), np.stack(halves(second.T.copy()))]),
    }


def split(value):
    high = value.astype(jnp.bfloat16)
    low = (value - high.astype(jnp.float32)).astype(jnp.bfloat16)
    return high, low


def dot(left, right):
    return jnp.dot(left, right, preferred_element_type=jnp.float32)


def swap_groups(vectors):
    group = lax.broadcasted_iota(jnp.int32, (8, 128), 1) // 8
    vectors = list(vectors)
    for bit in (1, 2, 4, 8):
        low = (group & bit) == 0
        for i in range(16):
            if i & bit:
                continue
            a, b = vectors[i], vectors[i | bit]
            vectors[i] = jnp.where(low, a, pltpu.roll(b, 8 * bit, 1))
            vectors[i | bit] = jnp.where(low, pltpu.roll(a, 128 - 8 * bit, 1), b)
    return vectors


def total_of(value):
    return jnp.sum(jnp.sum(value, axis=1, keepdims=True), axis=0, keepdims=True)


def project_and_send(weights, pert, zonal_t, proj, coef, spare, send):
    for level in range(LEV):
        for lt in range(LTILES):
            lanes = pl.ds(lt * 128, 128)
            fields = [
                jnp.concatenate([weights(v * LEV + level, rt, lt) for rt in range(TILES)], axis=0)
                for v in range(VARS)
            ]

            def member(k, carry, level=level, lanes=lanes, fields=fields):
                acc = pert[k, 0, level, :, lanes].astype(jnp.float32) * fields[0]
                for v in range(1, VARS):
                    acc = acc + pert[k, v, level, :, lanes].astype(jnp.float32) * fields[v]
                for rt in range(TILES):
                    at = pl.multiple_of(level * 240 + (rt * KLOC + k) * 8, 8)
                    proj[pl.ds(at, 8), lanes] = acc[rt * 8 : rt * 8 + 8]
                return carry

            lax.fori_loop(0, KLOC, member, 0, unroll=2)
    high, low = split(proj[...])
    result = dot(high, zonal_t[0]) + dot(low, zonal_t[0]) + dot(high, zonal_t[1])
    for level in range(LEV):
        coef[pl.ds(level * 256, 240), :] = result[level * 240 : level * 240 + 240]
        coef[pl.ds(level * 256 + 240, 16), :] = jnp.zeros((16, ZW), jnp.float32)
    if spare is not None:
        coef[pl.ds(240, 8), :] = jnp.broadcast_to(spare, (8, ZW))
    for level in range(LEV):
        for tile in range(2):
            for half in range(2):
                got = swap_groups(
                    coef[pl.ds(level * 256 + (tile * 16 + i) * 8, 8), pl.ds(half * 128, 128)]
                    for i in range(16)
                )
                for g in range(16):
                    send[half * 16 + g, pl.ds(level * 16 + tile * 8, 8), :] = got[g]


def first_kernel(pert, innovations, weight, zonal_t, send, proj, coef):
    def weights(c, rt, lt):
        at = (c // LEV, c % LEV, pl.ds(rt * 8, 8), pl.ds(lt * 128, 128))
        return weight[at] * innovations[at]

    project_and_send(weights, pert, zonal_t, proj, coef, None, send)


def assemble(me, parts, field):
    for j in range(RING):
        field[lax.rem(me - j + RING, RING)] = parts[j][pl.ds(0, CHUNK), :]


def own_columns(me, field, out):
    start = (3 * me) // 2
    odd = lax.rem(me, 2) == 1
    for c in range(RING):
        for rt in range(TILES):
            at = pl.multiple_of((rt * LTILES + start) * 8, 8)
            window = jnp.concatenate(
                [field[c, pl.ds(at, 8), :], field[c, pl.ds(at + 8, 8), :]], axis=1
            )
            window = jnp.where(odd, pltpu.roll(window, 192, 1), window)
            out[c // LEV, c % LEV, pl.ds(rt * 8, 8), :] = window[:, :SHARE]


def energy(weight, field):
    acc = jnp.zeros((8, 128), jnp.float32)
    for c in range(RING):
        for rt in range(TILES):
            for lt in range(LTILES):
                value = field[c, pl.ds((rt * LTILES + lt) * 8, 8), :]
                acc = acc + weight[
                    c // LEV, c % LEV, pl.ds(rt * 8, 8), pl.ds(lt * 128, 128)
                ] * (value * value)
    return total_of(acc)


def second_kernel(me_ref, pert, weight, zonal_t, *refs):
    parts, (send, field, own, scal, proj, coef) = refs[:RING], refs[RING:]
    me = me_ref[0]
    assemble(me, parts, field)
    own_columns(me, field, own)
    scal[...] = parts[0][pl.ds(CHUNK, 8), :]
    curve = energy(weight, field)

    def weights(c, rt, lt):
        at = (c // LEV, c % LEV, pl.ds(rt * 8, 8), pl.ds(lt * 128, 128))
        return weight[at] * field[c, pl.ds((rt * LTILES + lt) * 8, 8), :]

    project_and_send(weights, pert, zonal_t, proj, coef, curve, send)


def third_kernel(me_ref, pert, weight, zonal_t, old_scal, old_field, *refs):
    parts, (send, own, scal, proj, coef, field) = refs[:RING], refs[RING:]
    me = me_ref[0]
    norm = old_scal[0:1, 0:1]
    norm_next = parts[0][CHUNK : CHUNK + 1, 0:1]
    cross = parts[0][CHUNK + 1 : CHUNK + 2, 0:1]
    beta = norm_next / norm
    for j in range(RING):
        c = lax.rem(me - j + RING, RING)
        field[c] = parts[j][pl.ds(0, CHUNK), :] + beta * old_field[c]
    own_columns(me, field, own)
    square = norm_next + 2.0 * beta * cross + beta * beta * norm
    row = lax.broadcasted_iota(jnp.int32, (8, 128), 0)
    scal[...] = jnp.where(row == 0, norm_next, jnp.where(row == 1, square, beta))
    curve = energy(weight, field)

    def weights(c, rt, lt):
        at = (c // LEV, c % LEV, pl.ds(rt * 8, 8), pl.ds(lt * 128, 128))
        return weight[at] * field[c, pl.ds((rt * LTILES + lt) * 8, 8), :]

    project_and_send(weights, pert, zonal_t, proj, coef, curve, send)


def to_modes(received, level, merid_t):
    lane = lax.broadcasted_iota(jnp.int32, (MW, 128), 1)
    sums = []
    for tile in range(2):
        data = received[:, pl.ds(level * 16 + tile * 8, 8), :].reshape(BANDS * 8, 128)
        high, low = split(data)
        sums.append(
            dot(merid_t[tile, 0], high) + dot(merid_t[tile, 0], low) + dot(merid_t[tile, 1], high)
        )
    result = sums[0][:MW] + jnp.where(lane < 48, pltpu.roll(sums[0][MW:], 48, 1), 0.0)
    result = result + jnp.where(lane >= 48, pltpu.roll(sums[1][:MW], 48, 1), 0.0)
    result = result + pltpu.roll(sums[1][MW:], 96, 1)
    return jnp.where(lane < 80, result, 0.0)


def to_rows(value, merid, level, send, spares):
    lane = lax.broadcasted_iota(jnp.int32, (MW, 128), 1)
    moved = pltpu.roll(value, 80, 1)
    second = jnp.where(lane >= 80, moved, 0.0)
    third = jnp.where(lane < 32, moved, 0.0)
    fourth = pltpu.roll(value, 32, 1)
    for tile, pair in enumerate(((value, second), (third, fourth))):
        high, low = split(jnp.concatenate(pair, axis=0))
        rows = dot(merid[tile, 0], high) + dot(merid[tile, 0], low) + dot(merid[tile, 1], high)
        if tile == 1 and spares:
            row = lax.broadcasted_iota(jnp.int32, (BANDS * 8, 128), 0)
            column = lax.broadcasted_iota(jnp.int32, (BANDS * 8, 128), 1)
            top = (row % 8) == 0
            for position, spare in enumerate(spares):
                rows = rows + jnp.where(top & (column == 112 + 8 * position), spare, 0.0)
        send[:, pl.ds(level * 16 + tile * 8, 8), :] = rows.reshape(BANDS, 8, 128)


def spare_sum(received):
    data = received[:, pl.ds(8, 8), :].reshape(BANDS * 8, 128)
    row = lax.broadcasted_iota(jnp.int32, (BANDS * 8, 128), 0)
    column = lax.broadcasted_iota(jnp.int32, (BANDS * 8, 128), 1)
    return total_of(jnp.where(((row % 8) == 0) & (column == 112), data, 0.0))


def scale_of(localization):
    return jnp.concatenate([localization[...]] * 16, axis=0).T


def gradient_kernel(received, localization, merid_t, merid, send, gradient):
    scale = scale_of(localization)
    acc = jnp.zeros((MW, 128), jnp.float32)
    for level in range(LEV):
        value = to_modes(received, level, merid_t) * scale
        gradient[level] = value
        acc = acc + value * value
    norm = total_of(acc)
    for level in range(LEV):
        to_rows(gradient[level] * scale, merid, level, send, (norm,) if level == 0 else ())


def residual_kernel(received, localization, merid_t, merid, gradient, scal, send, residual, step_out):
    scale = scale_of(localization)
    norm = scal[0:1, 0:1]
    step = norm / (norm + spare_sum(received))
    step_out[...] = jnp.broadcast_to(step, (8, 128))
    squares = jnp.zeros((MW, 128), jnp.float32)
    cross = jnp.zeros((MW, 128), jnp.float32)
    for level in range(LEV):
        old = gradient[level]
        image = old + to_modes(received, level, merid_t) * scale
        value = old - step * image
        residual[level] = value
        squares = squares + value * value
        cross = cross + value * old
    spares = (total_of(squares), total_of(cross))
    for level in range(LEV):
        to_rows(residual[level] * scale, merid, level, send, spares if level == 0 else ())


def last_kernel(
    received, localization, merid_t, gradient, residual, scal, step_in, first_own, second_own,
    control_out, residual_out, increment_out,
):
    scale = scale_of(localization)
    norm_next, square, beta = scal[0:1, 0:1], scal[1:2, 0:1], scal[2:3, 0:1]
    first_step = step_in[0:1, 0:1]
    step = norm_next / (square + spare_sum(received))
    for level in range(LEV):
        old, res = gradient[level], residual[level]
        direction = res + beta * old
        image = direction + to_modes(received, level, merid_t) * scale
        for out, value in (
            (control_out, first_step * old + step * direction),
            (residual_out, res - step * image),
        ):
            turned = value.T
            for k in range(KLOC):
                out[k, level] = turned[k * 8 : k * 8 + 8]
    increment_out[...] = first_step[None, None] * first_own[...] + step[None, None] * second_own[...]


def synth_kernel(me_ref, received, pert, zonal, *refs):
    outs, (coef, amp, total) = refs[:RING], refs[RING:]
    me = me_ref[0]
    for level in range(LEV):
        for tile in range(2):
            for half in range(2):
                got = swap_groups(
                    received[half * 16 + g, pl.ds(level * 16 + tile * 8, 8), :] for g in range(16)
                )
                for i in range(16):
                    at = level * 256 + (tile * 16 + i) * 8
                    coef[pl.ds(at, 8), pl.ds(half * 128, 128)] = got[i]
    scalars = [total_of(coef[pl.ds(240 + 8 * i, 8), :]) for i in range(2)]
    high, low = split(jnp.concatenate([coef[pl.ds(0, 240), :], coef[pl.ds(256, 240), :]], axis=0))
    for part in range(LTILES // 2):
        wide = pl.ds(part * 256, 256)
        amp[...] = (
            dot(high, zonal[0, :, wide]) + dot(low, zonal[0, :, wide]) + dot(high, zonal[1, :, wide])
        )
        for level in range(LEV):
            for side in range(2):
                lt = part * 2 + side
                lanes = pl.ds(lt * 128, 128)

                def member(k, sums, level=level, side=side, lanes=lanes):
                    pieces = []
                    for rt in range(TILES):
                        at = pl.multiple_of(level * 240 + (rt * KLOC + k) * 8, 8)
                        pieces.append(amp[pl.ds(at, 8), pl.ds(side * 128, 128)])
                    field = jnp.concatenate(pieces, axis=0)
                    return tuple(
                        sums[v] + pert[k, v, level, :, lanes].astype(jnp.float32) * field
                        for v in range(VARS)
                    )

                zero = jnp.zeros((ROWS, 128), jnp.float32)
                sums = lax.fori_loop(0, KLOC, member, (zero,) * VARS, unroll=2)
                for v in range(VARS):
                    for rt in range(TILES):
                        total[v * LEV + level, pl.ds((rt * LTILES + lt) * 8, 8), :] = sums[v][
                            rt * 8 : rt * 8 + 8
                        ]
    row = lax.broadcasted_iota(jnp.int32, (8, 128), 0)
    extra = jnp.where(row == 0, scalars[0], jnp.where(row == 1, scalars[1], 0.0))
    for j in range(RING):
        outs[j][pl.ds(0, CHUNK), :] = total[lax.rem(me + j, RING)]
        outs[j][pl.ds(CHUNK, 8), :] = extra


def f32(*shape):
    return jax.ShapeDtypeStruct(shape, jnp.float32)


def call(kernel, outs, scratch, *args, scalars=0, flops=0):
    in_specs = [pl.BlockSpec(memory_space=pltpu.SMEM)] * scalars
    in_specs += [pl.BlockSpec(memory_space=pltpu.VMEM)] * (len(args) - scalars)
    moved = sum(math.prod(a.shape) * a.dtype.itemsize for a in args)
    return pl.pallas_call(
        kernel,
        out_shape=outs,
        in_specs=in_specs,
        out_specs=jax.tree.map(lambda _: pl.BlockSpec(memory_space=pltpu.VMEM), outs),
        scratch_shapes=scratch,
        compiler_params=pltpu.CompilerParams(vmem_limit_bytes=VMEM_LIMIT),
        cost_estimate=pl.CostEstimate(flops=flops, bytes_accessed=moved, transcendentals=0),
    )(*args)


def ring_permute(value, distance):
    return lax.ppermute(value, "member", [(i, (i + distance) % RING) for i in range(RING)])


def sum_members(outs):
    parts = [outs[0]] + [ring_permute(outs[j], j) for j in range(1, RING)]
    own = functools.reduce(lambda a, b: a + b, parts)
    return [own] + [ring_permute(own, j) for j in range(1, RING)]


def local(perturbations, innovations, error_weight, localization):
    const = {name: jnp.asarray(value) for name, value in bases().items()}
    me = lax.axis_index("member").astype(jnp.int32)[None]
    payload = f32(BANDS, 32, 128)
    vmem = lambda *shape: pltpu.VMEM(shape, jnp.float32)
    project_scratch = [vmem(480, NLON), vmem(512, ZW)]
    synth_scratch = [vmem(512, ZW), vmem(480, 256), vmem(RING, CHUNK, 128)]
    own = f32(VARS, LEV, ROWS, SHARE)
    modes = f32(LEV, MW, 128)
    field = f32(RING, CHUNK, 128)

    def exchange(value):
        return lax.all_to_all(value, "band", 0, 0)

    def synthesize(rows):
        outs = call(
            synth_kernel, [f32(CHUNK + 8, 128)] * RING, synth_scratch,
            me, rows, perturbations, const["zonal"], scalars=1, flops=1200000000,
        )
        return sum_members(outs)

    sent = call(
        first_kernel, payload, project_scratch,
        perturbations, innovations, error_weight, const["zonal_t"], flops=1200000000,
    )
    sent, gradient = call(
        gradient_kernel, [payload, modes], [],
        exchange(sent), localization, const["merid_t"], const["merid"], flops=200000000,
    )
    parts = synthesize(exchange(sent))
    sent, first_field, first_own, scal = call(
        second_kernel, [payload, field, own, f32(8, 128)], project_scratch,
        me, perturbations, error_weight, const["zonal_t"], *parts, scalars=1, flops=1200000000,
    )
    sent, residual, step = call(
        residual_kernel, [payload, modes, f32(8, 128)], [],
        exchange(sent), localization, const["merid_t"], const["merid"], gradient, scal,
        flops=200000000,
    )
    parts = synthesize(exchange(sent))
    sent, second_own, scal = call(
        third_kernel, [payload, own, f32(8, 128)], project_scratch + [vmem(RING, CHUNK, 128)],
        me, perturbations, error_weight, const["zonal_t"], scal, first_field, *parts,
        scalars=1, flops=1200000000,
    )
    return tuple(call(
        last_kernel,
        [f32(KLOC, LEV, ZW // BANDS, MW), f32(KLOC, LEV, ZW // BANDS, MW), own], [],
        exchange(sent), localization, const["merid_t"], gradient, residual, scal, step,
        first_own, second_own, flops=100000000,
    ))


def solution(mesh):
    return jax.shard_map(
        local,
        mesh=mesh,
        in_specs=(
            P("member", None, None, "band", None),
            P(None, None, "band", None),
            P(None, None, "band", None),
            P("band", None),
        ),
        out_specs=(
            P("member", None, "band", None),
            P("member", None, "band", None),
            P(None, None, "band", "member"),
        ),
        check_vma=False,
    )
```

time: 690 us -> 279 us (0.40)
  blocking collectives: 274 us -> 66.1 us
  local copies, waits for them, and re-layouts: 104 us -> 10.1 us
  waiting for transfers between devices: 162 us -> 96.8 us
  matrix products: 61.9 us -> 0 us
  starting transfers between devices: 20.3 us -> 72.7 us
  other arithmetic: 40.6 us -> 0.18 us
  Pallas kernels: 0 us -> 27.9 us
  between operations: 18.6 us -> 0.97 us
    psum x3 -> x0, blocking collectives: 221 us -> none  [the longest x2 147 us: squares(): return lax.psum(jnp.sum(vector * vector), ('member', 'band'))]
    psum x2 -> x0, waiting for transfers between devices: 139 us -> none  [local(): total = lax.psum(partial_sum, 'member')]
    ppermute x0 -> x28, waiting for transfers between devices: none -> 85.3 us  [ring_permute(): lax.ppermute(value, 'member', [(i, (i + distance) % RING) for i in range(...]
    ppermute x0 -> x28, starting transfers between devices: none -> 69 us  [ring_permute(): lax.ppermute(value, 'member', [(i, (i + distance) % RING) for i in range(...]
    dot_general x10 -> x0, matrix products: 61.9 us -> none  [the longest x3 26.8 us: analyse(): jnp.einsum('klyx,zx->klzy', projected, zonal, precision=HIGHEST_PRECISION)]
    unnamed x14 -> x28, local copies, waits for them, and re-layouts: 61.8 us -> 10.1 us
    pallas_call x0 -> x8, Pallas kernels: none -> 27.9 us  [call(): pl.pallas_call(kernel, out_shape=outs, in_specs=in_specs, out_specs=jax.t...]
    all_to_all x12 -> x0, local copies, waits for them, and re-layouts: 25.4 us -> none  [the longest x2 13 us: local(): lax.all_to_all(rows_out, 'band', split_axis=3, concat_axis=2, tiled=True)]
  transfers between devices with their start and end apart: 4 -> 29, of which waited for: 4 -> 17; matrix products, arithmetic and copies ran while one was open for 0% -> 0% of each run, Pallas kernels for 0% -> 0%
where the time goes in v1:
time: 279 us; the launch traced here: 275 us
  waiting for transfers between devices  96.8 us (35%)
  starting transfers between devices  72.7 us (26%)
  blocking collectives  66.1 us (24%)
  Pallas kernels  27.9 us (10%)
  local copies, waits for them, and re-layouts  10.1 us (4%)
    ppermute x28, waiting for transfers between devices, ring_permute(): lax.ppermute(value, 'member', [(i, (i + distance) % RING) for i in range(...  85.3 us
    ppermute x28, starting transfers between devices, ring_permute(): lax.ppermute(value, 'member', [(i, (i + distance) % RING) for i in range(...  69 us
    all_to_all x4, blocking collectives, exchange(): return lax.all_to_all(value, 'band', 0, 0)  66.1 us
    pallas_call x8, Pallas kernels, call(): pl.pallas_call(kernel, out_shape=outs, in_specs=in_specs, out_specs=jax.t...  27.9 us
    all_to_all x1, waiting for transfers between devices, exchange(): return lax.all_to_all(value, 'band', 0, 0)  11.6 us
    unnamed x28, local copies, waits for them, and re-layouts  10.1 us
  transfers between devices with their start and end apart: 29, of which 17 were waited for; matrix products, arithmetic and copies ran while one was open for 0% of the time, Pallas kernels for 0%

profile of v1, /device:TPU:1, one launch (start us, length us, event | category | flops | bytes accessed | tf_op | source)
XLA Modules:
  0.0 274.8 jit_solution(11328895877094805100)
XLA Ops:
  7.3 3.8 %shard_map.103 = f32[32,32,128]{2,1,0:T(8,128)S(1)} custom-call(bf16[10,4,2,24,1536]{4,3,2,1,0:T(8,128)(2,1)S(1)} %copy-done, f32[4,2,24,1536]{3,2,1,0:T(8,128)S(1)} %copy-done.9, f32[4,2,24,1536]{3,2,1,0:T(8,128)S(1)} %copy-done.4, bf16[2,1536,256]{2,1,0:T(8,128)(2,1)S(1)} %copy-done.2), custom_call_target="tpu_custom_call" | custom-call | flops 1200000000 | bytes 9830400 | tf_op jit(solution)/shard_map/pallas_call | solution.py:353
  11.0 20.0 %all_to_all.25.received = f32[32,32,128]{2,1,0:T(8,128)S(1)} all-to-all(f32[32,32,128]{2,1,0:T(8,128)S(1)} %shard_map.103), channel_id=1, replica_groups=mesh['member'=8,'band'=32] {'band'}, dimensions={0} | all-to-all | bytes 1048576 | tf_op jit(solution)/shard_map/all_to_all | solution.py:386
  33.0 3.7 %all-to-all-start.1 = ((f32[32,32,128]{2,1,0:T(8,128)}), f32[32,32,128]{2,1,0:T(8,128)S(1)}, u32[]{:S(2)}, u32[]{:S(2)}) async-start(f32[32,32,128]{2,1,0:T(8,128)} %copy-done.10), calls=%async_computation.1 | async-start | bytes 1048576 | tf_op jit(solution)/shard_map/all_to_all | solution.py:386
  36.7 11.6 %all-to-all-done.1.received = f32[32,32,128]{2,1,0:T(8,128)S(1)} async-done(((f32[32,32,128]{2,1,0:T(8,128)}), f32[32,32,128]{2,1,0:T(8,128)S(1)}, u32[]{:S(2)}, u32[]{:S(2)}) %all-to-all-start.1) | async-done | bytes 524320 | tf_op jit(solution)/shard_map/all_to_all | solution.py:386
  50.9 5.8 %shard_map.105 = (f32[296,128]{1,0:T(8,128)S(1)}, f32[296,128]{1,0:T(8,128)S(1)}, f32[296,128]{1,0:T(8,128)S(1)}, f32[296,128]{1,0:T(8,128)S(1)}, f32[296,128]{1...) custom-call(s32[1]{0:T(128)} %bitcast.me_ref, ...), custom_call_target="tpu_custom_call" | custom-call | flops 1200000000 | bytes 7995396 | tf_op jit(solution)/shard_map/pallas_call | solution.py:353
  61.4 3.8 %collective-permute-start.2 = (f32[296,128]{1,0:T(8,128)S(1)}, f32[296,128]{1,0:T(8,128)S(1)}, u32[]{:S(2)}, u32[]{:S(2)}) collective-permute-start(f32[296,128]{1,0:T(8,128)S(1)} %get-tuple-element.35), channel_id=1, source_target_pairs={{0,96},{32,128},{64,160},{96,192},{128,224},{160,0},{192,32},{224,... | collective-permute-start | bytes 454664 | tf_op jit(solution)/shard_map/ppermute | solution.py:365
  65.6 4.5 %collective-permute-start.4 = (f32[296,128]{1,0:T(8,128)S(1)}, f32[296,128]{1,0:T(8,128)S(1)}, u32[]{:S(2)}, u32[]{:S(2)}) collective-permute-start(f32[296,128]{1,0:T(8,128)S(1)} %get-tuple-element.37), channel_id=1, source_target_pairs={{0,160},{32,192},{64,224},{96,0},{128,32},{160,64},{192,96},{224,1... | collective-permute-start | bytes 454664 | tf_op jit(solution)/shard_map/ppermute | solution.py:365
  72.5 3.7 %collective-permute-start.6 = (f32[296,128]{1,0:T(8,128)S(1)}, f32[296,128]{1,0:T(8,128)S(1)}, u32[]{:S(2)}, u32[]{:S(2)}) collective-permute-start(f32[296,128]{1,0:T(8,128)S(1)} %get-tuple-element.39), channel_id=1, source_target_pairs={{0,224},{32,0},{64,32},{96,64},{128,96},{160,128},{192,160},{224,1... | collective-permute-start | bytes 454664 | tf_op jit(solution)/shard_map/ppermute | solution.py:365
  76.2 7.9 %collective-permute-done.2 = f32[296,128]{1,0:T(8,128)S(1)} collective-permute-done((f32[296,128]{1,0:T(8,128)S(1)}, f32[296,128]{1,0:T(8,128)S(1)}, u32[]{:S(2)}, u32[]{:S(2)}) %collective-permute-start.2) | collective-permute-done | bytes 151584 | tf_op jit(solution)/shard_map/ppermute | solution.py:365
  86.1 7.7 %collective-permute-done.5 = f32[296,128]{1,0:T(8,128)S(1)} collective-permute-done((f32[296,128]{1,0:T(8,128)S(1)}, f32[296,128]{1,0:T(8,128)S(1)}, u32[]{:S(2)}, u32[]{:S(2)}) %collective-permute-start.5) | collective-permute-done | bytes 151584 | tf_op jit(solution)/shard_map/ppermute | solution.py:365
  112.1 12.5 %collective-permute-done.9.refs_3_ = f32[296,128]{1,0:T(8,128)S(1)} collective-permute-done((f32[296,128]{1,0:T(8,128)S(1)}, f32[296,128]{1,0:T(8,128)S(1)}, u32[]{:S(2)}, u32[]{:S(2)}) %collective-permute-start.9) | collective-permute-done | bytes 151584 | tf_op jit(solution)/shard_map/ppermute | solution.py:365
  124.6 6.7 %collective-permute-done.7.refs_1_ = f32[296,128]{1,0:T(8,128)S(1)} collective-permute-done((f32[296,128]{1,0:T(8,128)S(1)}, f32[296,128]{1,0:T(8,128)S(1)}, u32[]{:S(2)}, u32[]{:S(2)}) %collective-permute-start.7) | collective-permute-done | bytes 151584 | tf_op jit(solution)/shard_map/ppermute | solution.py:365
  131.3 4.3 %shard_map.106 = (f32[32,32,128]{2,1,0:T(8,128)S(1)}, f32[8,288,128]{2,1,0:T(8,128)S(1)}, f32[4,2,24,192]{3,2,1,0:T(8,128)S(1)}, f32[8,128]{1,0:T(8,128)S(1)}) custom-call(s32[1]{0:T(128)} %bitcast.me_ref, bf16[10,4,2,24,1536]{4,3,2,1,0:T(8,128)(2,1)S(1)} %copy-done.1, f32[4,2,24,1536]{3,2,1,0:T(8,128)S(1)} %copy-done.5, ...), custom_call_target="tpu_custom_call" | custom-call | flops 1200000000 | bytes 9863172 | tf_op jit(solution)/shard_map/pallas_call | solution.py:353
  135.6 15.8 %all_to_all.26.received = f32[32,32,128]{2,1,0:T(8,128)S(1)} all-to-all(f32[32,32,128]{2,1,0:T(8,128)S(1)} %get-tuple-element.42), channel_id=1, replica_groups=mesh['member'=8,'band'=32] {'band'}, dimensions={0} | all-to-all | bytes 1048576 | tf_op jit(solution)/shard_map/all_to_all | solution.py:386
  152.5 15.0 %all_to_all.27.received = f32[32,32,128]{2,1,0:T(8,128)S(1)} all-to-all(f32[32,32,128]{2,1,0:T(8,128)S(1)} %get-tuple-element.44), channel_id=1, replica_groups=mesh['member'=8,'band'=32] {'band'}, dimensions={0} | all-to-all | bytes 1048576 | tf_op jit(solution)/shard_map/all_to_all | solution.py:386
  167.6 5.8 %shard_map.108 = (f32[296,128]{1,0:T(8,128)S(1)}, f32[296,128]{1,0:T(8,128)S(1)}, f32[296,128]{1,0:T(8,128)S(1)}, f32[296,128]{1,0:T(8,128)S(1)}, f32[296,128]{1...) custom-call(s32[1]{0:T(128)} %bitcast.me_ref, ...), custom_call_target="tpu_custom_call" | custom-call | flops 1200000000 | bytes 7995396 | tf_op jit(solution)/shard_map/pallas_call | solution.py:353
  173.4 9.4 %collective-permute-start.14 = (f32[296,128]{1,0:T(8,128)S(1)}, f32[296,128]{1,0:T(8,128)S(1)}, u32[]{:S(2)}, u32[]{:S(2)}) collective-permute-start(f32[296,128]{1,0:T(8,128)S(1)} %get-tuple-element.46), channel_id=1, source_target_pairs={{0,32},{32,64},{64,96},{96,128},{128,160},{160,192},{192,224},{224... | collective-permute-start | bytes 454664 | tf_op jit(solution)/shard_map/ppermute | solution.py:365
  194.1 5.3 %collective-permute-start.20 = (f32[296,128]{1,0:T(8,128)S(1)}, f32[296,128]{1,0:T(8,128)S(1)}, u32[]{:S(2)}, u32[]{:S(2)}) collective-permute-start(f32[296,128]{1,0:T(8,128)S(1)} %get-tuple-element.52), channel_id=1, source_target_pairs={{0,224},{32,0},{64,32},{96,64},{128,96},{160,128},{192,160},{224,1... | collective-permute-start | bytes 454664 | tf_op jit(solution)/shard_map/ppermute | solution.py:365
  199.4 9.2 %collective-permute-done.16 = f32[296,128]{1,0:T(8,128)S(1)} collective-permute-done((f32[296,128]{1,0:T(8,128)S(1)}, f32[296,128]{1,0:T(8,128)S(1)}, u32[]{:S(2)}, u32[]{:S(2)}) %collective-permute-start.16) | collective-permute-done | bytes 151584 | tf_op jit(solution)/shard_map/ppermute | solution.py:365
  208.7 6.9 %collective-permute-done.19 = f32[296,128]{1,0:T(8,128)S(1)} collective-permute-done((f32[296,128]{1,0:T(8,128)S(1)}, f32[296,128]{1,0:T(8,128)S(1)}, u32[]{:S(2)}, u32[]{:S(2)}) %collective-permute-start.19) | collective-permute-done | bytes 151584 | tf_op jit(solution)/shard_map/ppermute | solution.py:365
  235.8 10.6 %collective-permute-done.23.refs_3_ = f32[296,128]{1,0:T(8,128)S(1)} collective-permute-done((f32[296,128]{1,0:T(8,128)S(1)}, f32[296,128]{1,0:T(8,128)S(1)}, u32[]{:S(2)}, u32[]{:S(2)}) %collective-permute-start.23) | collective-permute-done | bytes 151584 | tf_op jit(solution)/shard_map/ppermute | solution.py:365
  246.5 6.8 %collective-permute-done.21.refs_1_ = f32[296,128]{1,0:T(8,128)S(1)} collective-permute-done((f32[296,128]{1,0:T(8,128)S(1)}, f32[296,128]{1,0:T(8,128)S(1)}, u32[]{:S(2)}, u32[]{:S(2)}) %collective-permute-start.21) | collective-permute-done | bytes 151584 | tf_op jit(solution)/shard_map/ppermute | solution.py:365
  253.3 4.6 %shard_map.109 = (f32[32,32,128]{2,1,0:T(8,128)S(1)}, f32[4,2,24,192]{3,2,1,0:T(8,128)S(1)}, f32[8,128]{1,0:T(8,128)S(1)}) custom-call(s32[1]{0:T(128)} %bitcast.me_ref, bf16[10,4,2,24,1536]{4,3,2,1,0:T(8,128)(2,1)S(1)} %bitcast.2, f32[4,2,24,1536]{3,2,1,0:T(8,128)S(1)} %copy-done.5, bf16[2,1536,256]{2,1,0:T(8,128)(2,1)S(1)} %copy-done.3, ...), custom_call_target="tpu_custom_call" | custom-call | flops 1200000000 | bytes 11046916 | tf_op jit(solution)/shard_map/pallas_call | solution.py:353
  257.9 15.3 %all_to_all.28.received = f32[32,32,128]{2,1,0:T(8,128)S(1)} all-to-all(f32[32,32,128]{2,1,0:T(8,128)S(1)} %get-tuple-element.53), channel_id=1, replica_groups=mesh['member'=8,'band'=32] {'band'}, dimensions={0} | all-to-all | bytes 1048576 | tf_op jit(solution)/shard_map/all_to_all | solution.py:386
  (77 shorter events, 73.2 us)
Async XLA Ops:
  33.0 15.3 %all-to-all-start.1 = ((f32[32,32,128]{2,1,0:T(8,128)}), f32[32,32,128]{2,1,0:T(8,128)S(1)}, u32[]{:S(2)}, u32[]{:S(2)}) async-start(f32[32,32,128]{2,1,0:T(8,128)} %copy-done.10), calls=%async_computation.1 | async-start | bytes 1048576 | tf_op jit(solution)/shard_map/all_to_all | solution.py:386
  56.7 13.4 %collective-permute-start = (f32[296,128]{1,0:T(8,128)S(1)}, f32[296,128]{1,0:T(8,128)S(1)}, u32[]{:S(2)}, u32[]{:S(2)}) collective-permute-start(f32[296,128]{1,0:T(8,128)S(1)} %get-tuple-element.33), channel_id=1, source_target_pairs={{0,32},{32,64},{64,96},{96,128},{128,160},{160,192},{192,224},{224... | collective-permute-start | bytes 454664 | tf_op jit(solution)/shard_map/ppermute | solution.py:365
  58.4 14.1 %collective-permute-start.1 = (f32[296,128]{1,0:T(8,128)S(1)}, f32[296,128]{1,0:T(8,128)S(1)}, u32[]{:S(2)}, u32[]{:S(2)}) collective-permute-start(f32[296,128]{1,0:T(8,128)S(1)} %get-tuple-element.34), channel_id=1, source_target_pairs={{0,64},{32,96},{64,128},{96,160},{128,192},{160,224},{192,0},{224,... | collective-permute-start | bytes 454664 | tf_op jit(solution)/shard_map/ppermute | solution.py:365
  61.4 22.7 %collective-permute-start.2 = (f32[296,128]{1,0:T(8,128)S(1)}, f32[296,128]{1,0:T(8,128)S(1)}, u32[]{:S(2)}, u32[]{:S(2)}) collective-permute-start(f32[296,128]{1,0:T(8,128)S(1)} %get-tuple-element.35), channel_id=1, source_target_pairs={{0,96},{32,128},{64,160},{96,192},{128,224},{160,0},{192,32},{224,... | collective-permute-start | bytes 454664 | tf_op jit(solution)/shard_map/ppermute | solution.py:365
  65.2 20.9 %collective-permute-start.3 = (f32[296,128]{1,0:T(8,128)S(1)}, f32[296,128]{1,0:T(8,128)S(1)}, u32[]{:S(2)}, u32[]{:S(2)}) collective-permute-start(f32[296,128]{1,0:T(8,128)S(1)} %get-tuple-element.36), channel_id=1, source_target_pairs={{0,128},{32,160},{64,192},{96,224},{128,0},{160,32},{192,64},{224,... | collective-permute-start | bytes 454664 | tf_op jit(solution)/shard_map/ppermute | solution.py:365
  65.6 20.4 %collective-permute-start.4 = (f32[296,128]{1,0:T(8,128)S(1)}, f32[296,128]{1,0:T(8,128)S(1)}, u32[]{:S(2)}, u32[]{:S(2)}) collective-permute-start(f32[296,128]{1,0:T(8,128)S(1)} %get-tuple-element.37), channel_id=1, source_target_pairs={{0,160},{32,192},{64,224},{96,0},{128,32},{160,64},{192,96},{224,1... | collective-permute-start | bytes 454664 | tf_op jit(solution)/shard_map/ppermute | solution.py:365
  70.1 23.7 %collective-permute-start.5 = (f32[296,128]{1,0:T(8,128)S(1)}, f32[296,128]{1,0:T(8,128)S(1)}, u32[]{:S(2)}, u32[]{:S(2)}) collective-permute-start(f32[296,128]{1,0:T(8,128)S(1)} %get-tuple-element.38), channel_id=1, source_target_pairs={{0,192},{32,224},{64,0},{96,32},{128,64},{160,96},{192,128},{224,1... | collective-permute-start | bytes 454664 | tf_op jit(solution)/shard_map/ppermute | solution.py:365
  72.5 21.8 %collective-permute-start.6 = (f32[296,128]{1,0:T(8,128)S(1)}, f32[296,128]{1,0:T(8,128)S(1)}, u32[]{:S(2)}, u32[]{:S(2)}) collective-permute-start(f32[296,128]{1,0:T(8,128)S(1)} %get-tuple-element.39), channel_id=1, source_target_pairs={{0,224},{32,0},{64,32},{96,64},{128,96},{160,128},{192,160},{224,1... | collective-permute-start | bytes 454664 | tf_op jit(solution)/shard_map/ppermute | solution.py:365
  97.1 14.2 %collective-permute-start.12 = (f32[296,128]{1,0:T(8,128)S(1)}, f32[296,128]{1,0:T(8,128)S(1)}, u32[]{:S(2)}, u32[]{:S(2)}) collective-permute-start(f32[296,128]{1,0:T(8,128)S(1)} %add_add_fusion.1.refs_0_), channel_id=1, source_target_pairs={{0,192},{32,224},{64,0},{96,32},{128,64},{160,96},{192,128},{224,1... | collective-permute-start | bytes 454664 | tf_op jit(solution)/shard_map/ppermute | solution.py:365
  98.0 14.1 %collective-permute-start.11 = (f32[296,128]{1,0:T(8,128)S(1)}, f32[296,128]{1,0:T(8,128)S(1)}, u32[]{:S(2)}, u32[]{:S(2)}) collective-permute-start(f32[296,128]{1,0:T(8,128)S(1)} %add_add_fusion.1.refs_0_), channel_id=1, source_target_pairs={{0,160},{32,192},{64,224},{96,0},{128,32},{160,64},{192,96},{224,1... | collective-permute-start | bytes 454664 | tf_op jit(solution)/shard_map/ppermute | solution.py:365
  102.5 22.1 %collective-permute-start.9 = (f32[296,128]{1,0:T(8,128)S(1)}, f32[296,128]{1,0:T(8,128)S(1)}, u32[]{:S(2)}, u32[]{:S(2)}) collective-permute-start(f32[296,128]{1,0:T(8,128)S(1)} %add_add_fusion.1.refs_0_), channel_id=1, source_target_pairs={{0,96},{32,128},{64,160},{96,192},{128,224},{160,0},{192,32},{224,... | collective-permute-start | bytes 454664 | tf_op jit(solution)/shard_map/ppermute | solution.py:365
  105.8 18.9 %collective-permute-start.8 = (f32[296,128]{1,0:T(8,128)S(1)}, f32[296,128]{1,0:T(8,128)S(1)}, u32[]{:S(2)}, u32[]{:S(2)}) collective-permute-start(f32[296,128]{1,0:T(8,128)S(1)} %add_add_fusion.1.refs_0_), channel_id=1, source_target_pairs={{0,64},{32,96},{64,128},{96,160},{128,192},{160,224},{192,0},{224,... | collective-permute-start | bytes 454664 | tf_op jit(solution)/shard_map/ppermute | solution.py:365
  111.3 20.0 %collective-permute-start.7 = (f32[296,128]{1,0:T(8,128)S(1)}, f32[296,128]{1,0:T(8,128)S(1)}, u32[]{:S(2)}, u32[]{:S(2)}) collective-permute-start(f32[296,128]{1,0:T(8,128)S(1)} %add_add_fusion.1.refs_0_), channel_id=1, source_target_pairs={{0,32},{32,64},{64,96},{96,128},{128,160},{160,192},{192,224},{224... | collective-permute-start | bytes 454664 | tf_op jit(solution)/shard_map/ppermute | solution.py:365
  173.4 20.6 %collective-permute-start.14 = (f32[296,128]{1,0:T(8,128)S(1)}, f32[296,128]{1,0:T(8,128)S(1)}, u32[]{:S(2)}, u32[]{:S(2)}) collective-permute-start(f32[296,128]{1,0:T(8,128)S(1)} %get-tuple-element.46), channel_id=1, source_target_pairs={{0,32},{32,64},{64,96},{96,128},{128,160},{160,192},{192,224},{224... | collective-permute-start | bytes 454664 | tf_op jit(solution)/shard_map/ppermute | solution.py:365
  184.2 24.4 %collective-permute-start.16 = (f32[296,128]{1,0:T(8,128)S(1)}, f32[296,128]{1,0:T(8,128)S(1)}, u32[]{:S(2)}, u32[]{:S(2)}) collective-permute-start(f32[296,128]{1,0:T(8,128)S(1)} %get-tuple-element.48), channel_id=1, source_target_pairs={{0,96},{32,128},{64,160},{96,192},{128,224},{160,0},{192,32},{224,... | collective-permute-start | bytes 454664 | tf_op jit(solution)/shard_map/ppermute | solution.py:365
  187.2 21.4 %collective-permute-start.17 = (f32[296,128]{1,0:T(8,128)S(1)}, f32[296,128]{1,0:T(8,128)S(1)}, u32[]{:S(2)}, u32[]{:S(2)}) collective-permute-start(f32[296,128]{1,0:T(8,128)S(1)} %get-tuple-element.49), channel_id=1, source_target_pairs={{0,128},{32,160},{64,192},{96,224},{128,0},{160,32},{192,64},{224,... | collective-permute-start | bytes 454664 | tf_op jit(solution)/shard_map/ppermute | solution.py:365
  188.6 20.0 %collective-permute-start.18 = (f32[296,128]{1,0:T(8,128)S(1)}, f32[296,128]{1,0:T(8,128)S(1)}, u32[]{:S(2)}, u32[]{:S(2)}) collective-permute-start(f32[296,128]{1,0:T(8,128)S(1)} %get-tuple-element.50), channel_id=1, source_target_pairs={{0,160},{32,192},{64,224},{96,0},{128,32},{160,64},{192,96},{224,1... | collective-permute-start | bytes 454664 | tf_op jit(solution)/shard_map/ppermute | solution.py:365
  194.0 21.6 %collective-permute-start.19 = (f32[296,128]{1,0:T(8,128)S(1)}, f32[296,128]{1,0:T(8,128)S(1)}, u32[]{:S(2)}, u32[]{:S(2)}) collective-permute-start(f32[296,128]{1,0:T(8,128)S(1)} %get-tuple-element.51), channel_id=1, source_target_pairs={{0,192},{32,224},{64,0},{96,32},{128,64},{160,96},{192,128},{224,1... | collective-permute-start | bytes 454664 | tf_op jit(solution)/shard_map/ppermute | solution.py:365
  194.1 22.4 %collective-permute-start.20 = (f32[296,128]{1,0:T(8,128)S(1)}, f32[296,128]{1,0:T(8,128)S(1)}, u32[]{:S(2)}, u32[]{:S(2)}) collective-permute-start(f32[296,128]{1,0:T(8,128)S(1)} %get-tuple-element.52), channel_id=1, source_target_pairs={{0,224},{32,0},{64,32},{96,64},{128,96},{160,128},{192,160},{224,1... | collective-permute-start | bytes 454664 | tf_op jit(solution)/shard_map/ppermute | solution.py:365
  220.7 15.2 %collective-permute-start.25 = (f32[296,128]{1,0:T(8,128)S(1)}, f32[296,128]{1,0:T(8,128)S(1)}, u32[]{:S(2)}, u32[]{:S(2)}) collective-permute-start(f32[296,128]{1,0:T(8,128)S(1)} %add_add_fusion.refs_0_), channel_id=1, source_target_pairs={{0,160},{32,192},{64,224},{96,0},{128,32},{160,64},{192,96},{224,1... | collective-permute-start | bytes 454664 | tf_op jit(solution)/shard_map/ppermute | solution.py:365
  222.5 13.4 %collective-permute-start.24 = (f32[296,128]{1,0:T(8,128)S(1)}, f32[296,128]{1,0:T(8,128)S(1)}, u32[]{:S(2)}, u32[]{:S(2)}) collective-permute-start(f32[296,128]{1,0:T(8,128)S(1)} %add_add_fusion.refs_0_), channel_id=1, source_target_pairs={{0,128},{32,160},{64,192},{96,224},{128,0},{160,32},{192,64},{224,... | collective-permute-start | bytes 454664 | tf_op jit(solution)/shard_map/ppermute | solution.py:365
  225.0 21.4 %collective-permute-start.23 = (f32[296,128]{1,0:T(8,128)S(1)}, f32[296,128]{1,0:T(8,128)S(1)}, u32[]{:S(2)}, u32[]{:S(2)}) collective-permute-start(f32[296,128]{1,0:T(8,128)S(1)} %add_add_fusion.refs_0_), channel_id=1, source_target_pairs={{0,96},{32,128},{64,160},{96,192},{128,224},{160,0},{192,32},{224,... | collective-permute-start | bytes 454664 | tf_op jit(solution)/shard_map/ppermute | solution.py:365
  227.1 19.4 %collective-permute-start.22 = (f32[296,128]{1,0:T(8,128)S(1)}, f32[296,128]{1,0:T(8,128)S(1)}, u32[]{:S(2)}, u32[]{:S(2)}) collective-permute-start(f32[296,128]{1,0:T(8,128)S(1)} %add_add_fusion.refs_0_), channel_id=1, source_target_pairs={{0,64},{32,96},{64,128},{96,160},{128,192},{160,224},{192,0},{224,... | collective-permute-start | bytes 454664 | tf_op jit(solution)/shard_map/ppermute | solution.py:365
  232.9 20.4 %collective-permute-start.21 = (f32[296,128]{1,0:T(8,128)S(1)}, f32[296,128]{1,0:T(8,128)S(1)}, u32[]{:S(2)}, u32[]{:S(2)}) collective-permute-start(f32[296,128]{1,0:T(8,128)S(1)} %add_add_fusion.refs_0_), channel_id=1, source_target_pairs={{0,32},{32,64},{64,96},{96,128},{128,160},{160,192},{192,224},{224... | collective-permute-start | bytes 454664 | tf_op jit(solution)/shard_map/ppermute | solution.py:365
  (19 other events, 457.6 us)
